TPU v7x, 32 devices: a whole 2x2x4 slice. The times are simulated.
32 devices in a mesh: parts: 2 (over y), blk: 16 (over z, x, core).
Axes of the slice: x: 2, y: 2, z: 4, core: 2. Of those that a mesh axis runs over, the one named last changes fastest.
Arguments:
- features: bfloat16 [8192, 128], P(('parts', 'blk')), parts along dimension 0, may hold values from -6 to 6
- w_first: bfloat16 [128, 256], replicated, may hold values from -0.5 to 0.5
- w_second: bfloat16 [256, 8192], replicated, may hold values from -0.375 to 0.375
- panel: bfloat16 [64, 64, 256], P(('parts', 'blk')), parts along dimension 0, may hold values from -6 to 6
- energies: float32 [256], replicated, may hold values from -1 to 1
- pair_dest: int32 [8192, 1], P(('parts', 'blk')), parts along dimension 0, may hold values from 0 to 15, as said below
- pair_row: int32 [8192], P(('parts', 'blk')), parts along dimension 0, may hold values from 0 to 1
- pair_col: int32 [8192], P(('parts', 'blk')), parts along dimension 0, may hold values from 0 to 1
Outputs:
- residual: float32 [64, 64, 256], P(('parts', 'blk')), parts along dimension 0
- loss: float32 [2], P('parts'), parts along dimension 0
- grad_first: float32 [256, 256], P('parts'), parts along dimension 0
- grad_second: float32 [512, 8192], P('parts', 'blk'), parts along dimension 0
There are 2 independent parts, one for each index of `parts`. A program takes and returns all parts, laid end to end along the dimension named above; an argument that names none is the same for every part. Nothing has to cross between parts.
Inputs may be any that keep to these rules, and one draw needn't show every extreme that they name: `pair_dest`: among one device's 256 pairs at most 24 have their block row on one device; every device owns the block rows of exactly 24 of its own pairs. Owners lie mostly near the listing device along the axis.
All inputs are finite; a program needn't handle non-finite values.
Results may differ from a plain program's by a relative error of at most 0.004.
Values may be sent and summed in bfloat16 or wider, within the bound.
A program may use at most 128 MiB of HBM per device.

v0:
```python
import jax
import jax.numpy as jnp
from jax import lax
from jax.sharding import PartitionSpec as P


def predict(feats, w_first, w_second, orbitals):
    pre = jnp.dot(feats, w_first, preferred_element_type=jnp.float32)
    hidden = jax.nn.silu(pre).astype(jnp.bfloat16)
    blocks = (jnp.dot(hidden, w_second, preferred_element_type=jnp.float32) / orbitals).astype(
        jnp.bfloat16
    )
    return (pre, hidden, blocks)


def weight_terms(feats, pre, hidden, d_flat, w_second, orbitals):
    term_second = jnp.dot(hidden.T, d_flat, preferred_element_type=jnp.float32) / orbitals
    d_hidden = (
        lax.dot_general(
            d_flat, w_second, (((1,), (1,)), ((), ())), preferred_element_type=jnp.float32
        )
        / orbitals
    )
    sig = jax.nn.sigmoid(pre)
    d_pre = (d_hidden * sig * (1.0 + pre * (1.0 - sig))).astype(jnp.bfloat16)
    term_first = jnp.dot(feats.T, d_pre, preferred_element_type=jnp.float32)
    return (term_first, term_second)


def slot_work(slot_blocks, slot_panel, slot_rows, energies, blk_dev, total_blocks):
    slots, unused_two, orbitals, unused_o = slot_blocks.shape
    columns = slot_panel.shape[2]
    group = 32
    steps_count = slots // group
    grouped = (
        slot_blocks.reshape(steps_count, group, 2, orbitals, orbitals),
        slot_panel.reshape(steps_count, group, orbitals, columns),
        slot_rows.reshape(steps_count, group),
    )
    row_ids = jnp.arange(blk_dev, dtype=jnp.int32)

    def forward(total, item):
        blocks, coeffs, rows = item
        h_panel = jnp.einsum(
            "sab,sbp->sap", blocks[:, 0], coeffs, preferred_element_type=jnp.float32
        )
        s_panel = jnp.einsum(
            "sab,sbp->sap", blocks[:, 1], coeffs, preferred_element_type=jnp.float32
        )
        contrib = h_panel - s_panel * energies
        selector = (rows[None, :] == row_ids[:, None]).astype(jnp.float32)
        added = jnp.einsum("rs,sap->rap", selector, contrib, precision=lax.Precision.HIGHEST)
        return (total + added, None)

    residual = lax.scan(forward, jnp.zeros((blk_dev, orbitals, columns), jnp.float32), grouped)[0]
    grad_h = (residual / total_blocks).astype(jnp.bfloat16)
    grad_s = (-(residual * energies) / total_blocks).astype(jnp.bfloat16)

    def backward(carry, item):
        blocks, coeffs, rows = item
        valid = (rows >= 0)[:, None, None]
        safe_rows = jnp.maximum(rows, 0)
        gh_rows = jnp.where(valid, grad_h[safe_rows], jnp.zeros((), jnp.bfloat16))
        gs_rows = jnp.where(valid, grad_s[safe_rows], jnp.zeros((), jnp.bfloat16))
        d_h = jnp.einsum(
            "sap,sbp->sab", gh_rows, coeffs, preferred_element_type=jnp.float32
        ).astype(jnp.bfloat16)
        d_s = jnp.einsum(
            "sap,sbp->sab", gs_rows, coeffs, preferred_element_type=jnp.float32
        ).astype(jnp.bfloat16)
        return (carry, jnp.stack([d_h, d_s], axis=1))

    d_blocks = lax.scan(backward, 0, grouped)[1]
    return (residual, d_blocks.reshape(slots, 2, orbitals, orbitals))


def local(features, w_first, w_second, panel, energies, pair_dest, pair_row, pair_col):
    n_dev = lax.axis_size("blk")
    my_index = lax.axis_index("blk")
    pair_count, feat_width = features.shape
    blk_dev, orbitals, columns = panel.shape
    capacity = 3 * pair_count // (2 * n_dev)
    slots = n_dev * capacity
    total_blocks = blk_dev * n_dev
    dest = pair_dest[:, 0]
    dest_table = (dest[:, None] == jnp.arange(n_dev, dtype=jnp.int32)[None, :]).astype(jnp.int32)
    rank_in = jnp.sum(jnp.cumsum(dest_table, axis=0) * dest_table, axis=1) - 1
    slot_of = dest * capacity + rank_in
    source = (
        jnp.full((slots,), pair_count, jnp.int32)
        .at[slot_of]
        .set(jnp.arange(pair_count, dtype=jnp.int32))
    )
    empty_label = jnp.full((1,), -1, jnp.int32)
    rows_sent = jnp.concatenate([pair_row, empty_label])[source]
    cols_sent = jnp.concatenate([my_index * blk_dev + pair_col, jnp.zeros((1,), jnp.int32)])[source]
    labels = jnp.stack([rows_sent, cols_sent], axis=-1).reshape(n_dev, capacity, 2)
    whole_panel = lax.all_gather(panel, "blk", axis=0, tiled=True)
    pre, hidden, blocks = predict(features, w_first, w_second, orbitals)
    padded = jnp.concatenate([blocks, jnp.zeros((1, blocks.shape[1]), jnp.bfloat16)], axis=0)
    send_blocks = padded[source].reshape(n_dev, capacity, 2, orbitals, orbitals)
    got_blocks, got_labels = (
        lax.all_to_all(send_blocks, "blk", split_axis=0, concat_axis=0, tiled=True),
        lax.all_to_all(labels, "blk", split_axis=0, concat_axis=0, tiled=True),
    )
    got_labels = got_labels.reshape(slots, 2)
    slot_panel = whole_panel[got_labels[:, 1]]
    residual, d_blocks = slot_work(
        got_blocks.reshape(slots, 2, orbitals, orbitals),
        slot_panel,
        got_labels[:, 0],
        energies,
        blk_dev,
        total_blocks,
    )
    back = lax.all_to_all(
        d_blocks.reshape(n_dev, capacity, 2, orbitals, orbitals),
        "blk",
        split_axis=0,
        concat_axis=0,
        tiled=True,
    )
    d_flat = back.reshape(slots, 2 * orbitals * orbitals)[slot_of]
    term_first, term_second = weight_terms(features, pre, hidden, d_flat, w_second, orbitals)
    grad_second = lax.psum_scatter(term_second, "blk", scatter_dimension=1, tiled=True)
    grad_first, square_sum = lax.psum((term_first, jnp.sum(residual * residual)), "blk")
    loss = (square_sum / (total_blocks * orbitals * columns)).reshape(1)
    return (residual, loss, grad_first, grad_second)


def solution(mesh):
    in_specs = (
        P(("parts", "blk"), None),
        P(),
        P(),
        P(("parts", "blk"), None, None),
        P(),
        P(("parts", "blk"), None),
        P(("parts", "blk")),
        P(("parts", "blk")),
    )
    out_specs = (P(("parts", "blk"), None, None), P("parts"), P("parts", None), P("parts", "blk"))
    return jax.shard_map(local, mesh=mesh, in_specs=in_specs, out_specs=out_specs, check_vma=False)
```

profile of v0, /device:TPU:0, one launch (start us, length us, event | category | flops | bytes accessed | tf_op | source)
XLA Modules:
  0.0 824.7 jit_solution(7765582669645620948)
XLA Ops:
  12.3 2.8 gather_fusion.3
  15.9 2.8 gather_fusion.2
  19.4 7.4 all-to-all-start
  27.8 3.5 fusion.35
  31.3 2.5 concatenate.12
  33.7 17.6 %gather_fusion.4 = bf16[384,8192]{1,0:T(8,128)(2,1)} fusion(bf16[257,8192]{1,0:T(8,128)(2,1)} %concatenate.12, s32[1024]{0:T(1024)S(1)} %pad_clamp_fusion.3), kind=kCustom, calls=%fused_computation.4 | custom fusion | bytes 12584448 | tf_op jit(solution)/shard_map/gather | solution.py:101
  51.4 17.9 %reshape.77 = bf16[16,24,2,64,64]{4,3,2,1,0:T(8,128)(2,1)} reshape(bf16[384,8192]{1,0:T(8,128)(2,1)} %gather_fusion.4) | data formatting | bytes 12582912 | tf_op jit(solution)/shard_map/reshape | solution.py:101
  69.2 16.7 %reshape.156 = bf16[16,2,98304]{2,1,0:T(2,128)(2,1)} reshape(bf16[16,24,2,64,64]{4,3,2,1,0:T(8,128)(2,1)} %reshape.77) | data formatting | bytes 12582912
  85.9 6.0 all-to-all-start.1
  92.9 98.0 %all-gather.2.cloned.1.call-done = bf16[32,64,256]{2,1,0:T(8,128)(2,1)} async-done(((bf16[2,64,256]{2,1,0:T(8,128)(2,1)}), bf16[32,64,256]{2,1,0:T(8,128)(2,1)}) %all-gather.2.cloned.1.call-update) | async-done | bytes 1048592 | tf_op jit(solution)/shard_map/all_gather | solution.py:98
  191.0 12.4 %gather_fusion.5 = bf16[384,64,256]{2,1,0:T(8,128)(2,1)} fusion(bf16[32,64,256]{2,1,0:T(8,128)(2,1)} %all-gather.2.cloned.1.call-done, s32[1024]{0:T(1024)S(1)} %pad_clamp_fusion.2), kind=kCustom, calls=%fused_computation.5 | custom fusion | bytes 25167360 | tf_op jit(solution)/shard_map/gather | solution.py:107
  203.4 9.1 %all-to-all-done.1 = bf16[16,2,98304]{2,1,0:T(2,128)(2,1)} async-done(((bf16[16,2,98304]{2,1,0:T(2,128)(2,1)}), bf16[16,2,98304]{2,1,0:T(2,128)(2,1)}, u32[]{:S(2)}, u32[]{:S(2)}) %all-to-all-start.1) | async-done | bytes 6291488 | tf_op jit(solution)/shard_map/all_to_all | solution.py:103
  212.5 16.4 %reshape.157 = bf16[16,24,2,64,64]{4,3,2,1,0:T(8,128)(2,1)} reshape(bf16[16,2,98304]{2,1,0:T(2,128)(2,1)} %all-to-all-done.1) | data formatting | bytes 12582912
  229.0 82.3 %while.22 = (s32[]{:T(128)}, f32[2,64,256]{2,0,1:T(2,128)S(1)}, s32[12,32]{1,0:T(8,128)S(1)}, bf16[12,32,2,64,64]{4,3,2,1,0:T(8,128)(2,1)}, bf16[12,32,64,256]{3...) while((s32[]{:T(128)}, f32[2,64,256]{2,0,1:T(2,128)S(1)}, ...), condition=%wide.region_5.6_spmd.clone, body=%wide.region_4.5_spmd.clone.sunk | while | flops 147914816 | bytes 13372387 | solution.py:55
  233.6 2.2 fusion.85
  240.5 2.2 fusion.85
  247.3 2.2 fusion.85
  254.2 2.2 fusion.85
  261.1 2.2 fusion.85
  267.9 2.2 fusion.85
  274.8 2.2 fusion.85
  281.7 2.2 fusion.85
  288.5 2.2 fusion.85
  295.4 2.2 fusion.85
  302.3 2.2 fusion.85
  309.1 2.2 fusion.85
  312.1 72.8 %while.21 = (s32[]{:T(128)}, bf16[12,32,2,64,64]{4,3,2,1,0:T(8,128)(2,1)}, s32[12,32]{1,0:T(8,128)S(1)}, bf16[2,64,256]{2,1,0:T(8,128)(2,1)S(1)}, bf16[12,32,64,...) while((s32[]{:T(128)}, bf16[12,32,2,64,64]{4,3,2,1,0:T(8,128)(2,1)}, ...), condition=%wide.region_9.10_spmd, body=%wide.region_8.9_spmd.sunk | while | flops 135791680 | bytes 10492341 | solution.py:73
  321.2 1.7 fusion.78
  327.3 1.7 fusion.78
  333.3 1.7 fusion.78
  339.4 1.7 fusion.78
  351.5 1.7 fusion.78
  367.3 1.7 fusion.77
  369.6 1.7 fusion.78
  373.4 1.7 fusion.77
  375.7 1.7 fusion.78
  379.4 1.7 fusion.77
  384.8 16.6 %reshape.158 = bf16[16,2,98304]{2,1,0:T(2,128)(2,1)} reshape(bf16[16,24,2,64,64]{4,3,2,1,0:T(8,128)(2,1)} %bitcast.100) | data formatting | bytes 12582912
  401.5 28.0 %all-to-all-start.2 = ((bf16[16,2,98304]{2,1,0:T(2,128)(2,1)}), bf16[16,2,98304]{2,1,0:T(2,128)(2,1)}, u32[]{:S(2)}, u32[]{:S(2)}) async-start(bf16[16,2,98304]{2,1,0:T(2,128)(2,1)} %reshape.158), calls=%async_computation.2 | async-start | bytes 12582912 | tf_op jit(solution)/shard_map/all_to_all | solution.py:116
  429.9 113.9 %all-to-all-done.2 = bf16[16,2,98304]{2,1,0:T(2,128)(2,1)} async-done(((bf16[16,2,98304]{2,1,0:T(2,128)(2,1)}), bf16[16,2,98304]{2,1,0:T(2,128)(2,1)}, u32[]{:S(2)}, u32[]{:S(2)}) %all-to-all-start.2) | async-done | bytes 6291488 | tf_op jit(solution)/shard_map/all_to_all | solution.py:116
  543.7 16.3 %reshape.159 = bf16[16,24,2,64,64]{4,3,2,1,0:T(8,128)(2,1)} reshape(bf16[16,2,98304]{2,1,0:T(2,128)(2,1)} %all-to-all-done.2) | data formatting | bytes 12582912
  560.0 17.0 %reshape.80 = bf16[384,8192]{1,0:T(8,128)(2,1)} reshape(bf16[16,24,2,64,64]{4,3,2,1,0:T(8,128)(2,1)} %reshape.159) | data formatting | bytes 12582912 | tf_op jit(solution)/shard_map/reshape | solution.py:123
  577.0 12.6 %gather_fusion.6 = bf16[256,8192]{1,0:T(8,128)(2,1)} fusion(bf16[384,8192]{1,0:T(8,128)(2,1)} %reshape.80, s32[1024]{0:T(1024)S(1)} %pad_clamp_fusion.1), kind=kCustom, calls=%fused_computation.6 | custom fusion | bytes 8389632 | tf_op jit(solution)/shard_map/gather | solution.py:123
  589.6 5.7 convolution_bitcast_fusion
  595.3 6.7 convolution_multiply_fusion
  602.1 56.7 %psum.14 = f32[]{:T(128)} all-reduce(f32[]{:T(128)} %get-tuple-element.172), channel_id=1, replica_groups=mesh['parts'=2,'blk'=16] {'blk'}, use_global_device_ids=true, to_apply=%region_7.8 | all-reduce | flops 1 | bytes 8 | tf_op jit(solution)/shard_map/psum | solution.py:126
  660.1 45.8 %all-reduce.3.cloned.1.call-done = f32[128,256]{0,1:T(8,128)} async-done(((f32[128,256]{0,1:T(8,128)}), f32[128,256]{0,1:T(8,128)}) %all-reduce.3.cloned.1.call-update) | async-done | bytes 131088 | tf_op jit(solution)/shard_map/psum | solution.py:126
  707.6 109.5 %reduce-scatter.2.cloned.1.call-done = f32[256,512]{1,0:T(8,128)} async-done(((f32[256,8192]{1,0:T(8,128)}), f32[256,512]{1,0:T(8,128)}) %reduce-scatter.2.cloned.1.call-update) | async-done | bytes 524304 | tf_op jit(solution)/shard_map/reduce_scatter | solution.py:125
  (177 shorter events, 122.7 us)
Async XLA Ops:
  7.2 19.6 %copy-start = (bf16[256,128]{1,0:T(8,128)(2,1)S(1)}, bf16[256,128]{1,0:T(8,128)(2,1)}, u32[]{:S(2)}) copy-start(bf16[256,128]{1,0:T(8,128)(2,1)} %param.12) | copy-start | bytes 196612
  19.4 66.5 %all-to-all-start = ((s32[16,24,2]{1,2,0:T(2,128)}), s32[16,24,2]{1,2,0:T(2,128)S(1)}, u32[]{:S(2)}, u32[]{:S(2)}) async-start(s32[16,24,2]{1,2,0:T(2,128)} %pad_add_fusion), calls=%async_computation | async-start | bytes 32768 | tf_op jit(solution)/shard_map/all_to_all | solution.py:104
  85.9 126.6 %all-to-all-start.1 = ((bf16[16,2,98304]{2,1,0:T(2,128)(2,1)}), bf16[16,2,98304]{2,1,0:T(2,128)(2,1)}, u32[]{:S(2)}, u32[]{:S(2)}) async-start(bf16[16,2,98304]{2,1,0:T(2,128)(2,1)} %reshape.156), calls=%async_computation.1 | async-start | bytes 12582912 | tf_op jit(solution)/shard_map/all_to_all | solution.py:103
  92.0 99.0 %all-gather.2.cloned.1.call-start = ((), (), s32[]{:S(2)}) async-start(), calls=%async_computation.4 | async-start | bytes 1114112 | tf_op jit(solution)/shard_map/all_gather | solution.py:98
  203.4 25.6 %copy-start.1 = (f32[256]{0:T(256)S(1)}, f32[256]{0:T(256)}, u32[]{:S(2)}) copy-start(f32[256]{0:T(256)} %param.16) | copy-start | bytes 3076
  401.5 142.2 %all-to-all-start.2 = ((bf16[16,2,98304]{2,1,0:T(2,128)(2,1)}), bf16[16,2,98304]{2,1,0:T(2,128)(2,1)}, u32[]{:S(2)}, u32[]{:S(2)}) async-start(bf16[16,2,98304]{2,1,0:T(2,128)(2,1)} %reshape.158), calls=%async_computation.2 | async-start | bytes 12582912 | tf_op jit(solution)/shard_map/all_to_all | solution.py:116
  429.5 276.4 %all-reduce.3.cloned.1.call-start = ((), (), s32[]{:S(2)}) async-start(), calls=%async_computation.5 | async-start | bytes 262144 | tf_op jit(solution)/shard_map/psum | solution.py:126
  595.3 221.8 %reduce-scatter.2.cloned.1.call-start = ((), (), s32[]{:S(2)}) async-start(), calls=%async_computation.6 | async-start | bytes 8912896 | tf_op jit(solution)/shard_map/reduce_scatter | solution.py:125
Sparse Core Ops, SparseCore 0:
  95.0 95.9 all-gather.1
  595.4 110.4 all-reduce.2
  710.5 106.4 reduce-scatter.1
where the time goes:
time: 830 us; the launch traced here: 825 us
  waiting for transfers between devices  377 us (45%)
  local copies, waits for them, and re-layouts  186 us (22%)
  matrix products  124 us (15%)
  blocking collectives  56.7 us (7%)
  starting transfers between devices  42.1 us (5%)
  other arithmetic  21.9 us (3%)
  between operations  15.7 us (2%)
    all_to_all x1, waiting for transfers between devices, local(): lax.all_to_all(d_blocks.reshape(n_dev, capacity, 2, orbitals, orbitals),...  114 us
    reduce_scatter x1, waiting for transfers between devices, local(): lax.psum_scatter(term_second, 'blk', scatter_dimension=1, tiled=True)  109 us
    all_gather x1, waiting for transfers between devices, local(): whole_panel = lax.all_gather(panel, 'blk', axis=0, tiled=True)  98 us
    unnamed x10, local copies, waits for them, and re-layouts  68.4 us
    psum x1, blocking collectives, local(): lax.psum((term_first, jnp.sum(residual * residual)), 'blk')  56.7 us
    psum x1, waiting for transfers between devices, local(): lax.psum((term_first, jnp.sum(residual * residual)), 'blk')  45.8 us
    all_to_all x1, starting transfers between devices, local(): lax.all_to_all(d_blocks.reshape(n_dev, capacity, 2, orbitals, orbitals),...  28 us
    dot_general x12, matrix products, forward(): jnp.einsum('rs,sap->rap', selector, contrib, precision=lax.Precision.HIGH...  26.3 us
  transfers between devices with their start and end apart: 6, of which 5 were waited for; matrix products, arithmetic and copies ran while one was open for 10% of the time, Pallas kernels for 0%

commit v1 on v0

--- a/solution.py
+++ b/solution.py
@@ -128,6 +128,55 @@
     return (residual, loss, grad_first, grad_second)
 
 
+def fast_local(features, w_first, w_second, panel, energies, pair_dest, pair_row, pair_col):
+    n_dev = lax.axis_size("blk")
+    me = lax.axis_index("blk")
+    pairs, width = features.shape
+    blk_dev, orbitals, columns = panel.shape
+    hid = w_second.shape[0]
+    blocks = blk_dev * n_dev
+    groups = blk_dev * blocks
+    half = n_dev // 2
+    a_count = orbitals // half
+    side = me // half
+    spot = me % half
+    f32 = jnp.float32
+    gid = pair_col * blocks + pair_dest[:, 0] * blk_dev + pair_row
+    feats = lax.all_gather(features, "blk", axis=0, tiled=True)
+    gids = lax.all_gather(gid, "blk", axis=0, tiled=False)
+    coeffs = lax.all_gather(panel, "blk", axis=0, tiled=True)
+    pre = jnp.dot(feats, w_first, preferred_element_type=f32)
+    sig = jax.nn.sigmoid(pre)
+    hidden = (pre * sig).astype(jnp.bfloat16)
+    onehot = (gids[:, None, :] == jnp.arange(groups, dtype=jnp.int32)[None, :, None]).astype(jnp.bfloat16)
+    summed = jnp.einsum("dgp,dpk->dgk", onehot, hidden.reshape(n_dev, pairs, hid), preferred_element_type=f32)
+    summed = summed.astype(jnp.bfloat16).reshape(n_dev * groups, hid)
+    w_sides = w_second.reshape(hid, 2, orbitals * orbitals)
+    w_part = lax.dynamic_slice_in_dim(w_sides, spot * a_count * orbitals, a_count * orbitals, 2)
+    w_own = lax.dynamic_index_in_dim(w_part, side, 1, keepdims=False)
+    mats = jnp.dot(summed, w_part.reshape(hid, -1), preferred_element_type=f32) / orbitals
+    mats = mats.astype(jnp.bfloat16).reshape(blocks, blocks, 2, a_count, orbitals)
+    both = jnp.einsum("crhab,cbp->hrap", mats, coeffs, preferred_element_type=f32)
+    resid = both[0] - both[1] * energies
+    grad = jnp.where(side == 0, resid / blocks, -(resid * energies) / blocks).astype(jnp.bfloat16)
+    d_mats = jnp.einsum("rap,cbp->crab", grad, coeffs, preferred_element_type=f32)
+    d_mats = d_mats.astype(jnp.bfloat16).reshape(blocks * blocks, a_count * orbitals)
+    grad_second = jnp.dot(summed.T, d_mats, preferred_element_type=f32) / orbitals
+    d_sum = lax.dot_general(d_mats, w_own, (((1,), (1,)), ((), ())), preferred_element_type=f32) / orbitals
+    d_sum = d_sum.astype(jnp.bfloat16).reshape(n_dev, groups, hid)
+    d_hidden = jnp.einsum("dgp,dgk->dpk", onehot, d_sum, preferred_element_type=f32).reshape(-1, hid)
+    d_pre = (d_hidden * sig * (1.0 + pre * (1.0 - sig))).astype(jnp.bfloat16)
+    term_first = jnp.dot(feats.T, d_pre, preferred_element_type=f32)
+    mine = lax.dynamic_slice_in_dim(resid, side * (blocks // 2), blocks // 2, 0)
+    mine = mine.reshape(half, blk_dev, a_count, columns)
+    sides = [list(range(half)), list(range(half, n_dev))]
+    got = lax.all_to_all(mine, "blk", 0, 0, axis_index_groups=sides, tiled=True)
+    residual = got.transpose(1, 0, 2, 3).reshape(blk_dev, orbitals, columns)
+    grad_first, square_sum = lax.psum((term_first, 0.5 * jnp.sum(resid * resid)), "blk")
+    loss = (square_sum / (blocks * orbitals * columns)).reshape(1)
+    return (residual, loss, grad_first, grad_second)
+
+
 def solution(mesh):
     in_specs = (
         P(("parts", "blk"), None),
@@ -140,4 +189,5 @@
         P(("parts", "blk")),
     )
     out_specs = (P(("parts", "blk"), None, None), P("parts"), P("parts", None), P("parts", "blk"))
-    return jax.shard_map(local, mesh=mesh, in_specs=in_specs, out_specs=out_specs, check_vma=False)
+    return jax.shard_map(
+        fast_local if mesh.shape["blk"] <= 32 else local, mesh=mesh, in_specs=in_specs, out_specs=out_specs, check_vma=False)

time: 830 us -> 201 us (0.24)
  waiting for transfers between devices: 377 us -> 89 us
  local copies, waits for them, and re-layouts: 186 us -> 17.3 us
  matrix products: 124 us -> 15.2 us
  starting transfers between devices: 42.1 us -> 3.49 us
  other arithmetic: 21.9 us -> 2.5 us
    all_to_all x3 -> x1, waiting for transfers between devices: 123 us -> 0.01 us  [fast_local(): got = lax.all_to_all(mine, 'blk', 0, 0, axis_index_groups=sides, tiled=True)]
    reduce_scatter x1 -> x0, waiting for transfers between devices: 109 us -> none  [local(): lax.psum_scatter(term_second, 'blk', scatter_dimension=1, tiled=True)]
    dot_general x64 -> x9, matrix products: 124 us -> 15.2 us  [the longest x1 4.33 us: fast_local(): pre = jnp.dot(feats, w_first, preferred_element_type=f32)]
    gather x29 -> x0, local copies, waits for them, and re-layouts: 62.9 us -> none  [the longest x1 17.6 us: local(): send_blocks = padded[source].reshape(n_dev, capacity, 2, orbitals, orbitals)]
    unnamed x10 -> x21, local copies, waits for them, and re-layouts: 68.4 us -> 8.14 us
    all_gather x1 -> x2, waiting for transfers between devices: 98 us -> 40.9 us  [the longest x1 29.5 us: fast_local(): coeffs = lax.all_gather(panel, 'blk', axis=0, tiled=True)]
    all_to_all x3 -> x1, starting transfers between devices: 41.5 us -> 3.37 us  [fast_local(): got = lax.all_to_all(mine, 'blk', 0, 0, axis_index_groups=sides, tiled=True)]
    reshape x3, local copies, waits for them, and re-layouts: 35 us -> 6.83 us  [the longest x1 4.08 us: fast_local(): mats.astype(jnp.bfloat16).reshape(blocks, blocks, 2, a_count, orbitals)]
  transfers between devices with their start and end apart: 6 -> 4, of which waited for: 5 -> 3; matrix products, arithmetic and copies ran while one was open for 10% -> 10% of each run, Pallas kernels for 0% -> 0%
where the time goes in v1:
time: 201 us; the launch traced here: 200 us
  waiting for transfers between devices  89 us (44%)
  blocking collectives  55.9 us (28%)
  local copies, waits for them, and re-layouts  17.3 us (9%)
  between operations  16.4 us (8%)
  matrix products  15.2 us (8%)
  starting transfers between devices  3.49 us (2%)
  other arithmetic  2.5 us (1%)
    psum x1, waiting for transfers between devices, fast_local(): lax.psum((term_first, 0.5 * jnp.sum(resid * resid)), 'blk')  46.6 us
    psum x1, blocking collectives, fast_local(): lax.psum((term_first, 0.5 * jnp.sum(resid * resid)), 'blk')  32.8 us
    all_gather x1, waiting for transfers between devices, fast_local(): coeffs = lax.all_gather(panel, 'blk', axis=0, tiled=True)  29.5 us
    all_gather x1, blocking collectives, fast_local(): gids = lax.all_gather(gid, 'blk', axis=0, tiled=False)  23.1 us
    all_gather x1, waiting for transfers between devices, fast_local(): feats = lax.all_gather(features, 'blk', axis=0, tiled=True)  11.4 us
    unnamed x21, local copies, waits for them, and re-layouts  8.14 us
    dot_general x1, matrix products, fast_local(): pre = jnp.dot(feats, w_first, preferred_element_type=f32)  4.33 us
    reshape x1, local copies, waits for them, and re-layouts, fast_local(): mats.astype(jnp.bfloat16).reshape(blocks, blocks, 2, a_count, orbitals)  4.08 us
  transfers between devices with their start and end apart: 4, of which 3 were waited for; matrix products, arithmetic and copies ran while one was open for 10% of the time, Pallas kernels for 0%

profile of v1, /device:TPU:0, one launch (start us, length us, event | category | flops | bytes accessed | tf_op | source)
XLA Modules:
  0.0 199.8 jit_solution(2431973810844996383)
XLA Ops:
  7.2 0.0 copy-start
  7.2 0.0 all-gather.5.cloned.1.call-start
  7.2 0.7 all-gather.5.cloned.1.call-update
  7.9 0.0 all-gather.7.cloned.1.call-start
  8.0 0.7 all-gather.7.cloned.1.call-update
  8.7 0.0 all-reduce.2.cloned.1.call-start
  8.7 0.0 copy-start.6
  8.8 0.0 copy-start.7
  8.8 0.0 copy-start.8
  8.8 6.4 %copy.25 = bf16[256,8192]{0,1:T(8,128)(2,1)} copy(bf16[256,8192]{1,0:T(8,128)(2,1)} %param.10) | data formatting | bytes 8388608 | tf_op args[2]
  15.2 0.0 copy-done.6
  15.2 0.0 copy-done.7
  15.2 0.0 copy-done.8
  15.2 23.1 %all-gather.1 = s32[16,1,256]{2,1,0:T(1,128)S(1)} all-gather(s32[1,1,256]{2,1,0:T(1,128)S(1)} %bitcast.86), channel_id=2, replica_groups=mesh['parts'=2,'blk'=16] {'blk'}, dimensions={0}, use_global_device_ids=true | all-gather | bytes 17408 | tf_op jit(solution)/shard_map/all_gather | solution.py:146
  38.3 1.1 constant_dynamic-slice_fusion.1
  39.4 11.4 %all-gather.5.cloned.1.call-done = bf16[4096,128]{1,0:T(8,128)(2,1)} async-done(((bf16[256,128]{1,0:T(8,128)(2,1)}), bf16[4096,128]{1,0:T(8,128)(2,1)}) %all-gather.5.cloned.1.call-update) | async-done | bytes 1048592 | tf_op jit(solution)/shard_map/all_gather | solution.py:145
  50.8 0.0 copy-done
  50.9 4.3 %multiply_convert_fusion.1 = (bf16[4096,256]{1,0:T(8,128)(2,1)S(1)}, f32[4096,256]{1,0:T(8,128)}) fusion(bf16[4096,128]{1,0:T(8,128)(2,1)} %all-gather.5.cloned.1.call-done, bf16[128,256]{1,0:T(8,128)(2,1)S(1)} %copy-done), kind=kOutput, calls=%fused_computation.6 | convolution fusion | flops 273678336 | bytes 7405568 | tf_op jit(solution)/shard_map/dot_general | solution.py:148
  55.2 0.4 convolution_convert_fusion
  55.6 0.7 multiply_convert_fusion
  56.3 4.1 %reshape.49 = bf16[32,32,2,8,64]{4,3,2,1,0:T(8,128)(2,1)} reshape(bf16[1024,1024]{1,0:T(8,128)(2,1)S(1)} %multiply_convert_fusion) | data formatting | bytes 4194304 | tf_op jit(solution)/shard_map/reshape | solution.py:158
  60.4 29.5 %all-gather.7.cloned.1.call-done = bf16[32,64,256]{2,1,0:T(8,128)(2,1)} async-done(((bf16[2,64,256]{2,1,0:T(8,128)(2,1)}), bf16[32,64,256]{2,1,0:T(8,128)(2,1)}) %all-gather.7.cloned.1.call-update) | async-done | bytes 1048592 | tf_op jit(solution)/shard_map/all_gather | solution.py:147
  89.9 3.7 %fusion.2 = f32[32,2,8,256,1]{3,2,0,1,4:T(8,128)S(1)} fusion(bf16[32,32,2,8,64]{4,3,2,1,0:T(8,128)(2,1)} %reshape.49, bf16[32,64,256]{2,1,0:T(8,128)(2,1)} %all-gather.7.cloned.1.call-done), kind=kOutput, calls=%fused_computation.3 | convolution fusion | flops 536870912 | bytes 3670016 | tf_op jit(solution)/shard_map/crhab,cbp->hrap/dot_general | solution.py:159
  93.6 0.1 copy.42
  93.7 0.0 copy-done.5
  93.7 0.7 multiply_reduce_fusion
  94.3 0.0 copy-done.4
  94.3 0.7 convert_bitcast_fusion
  95.1 0.6 copy.28
  95.7 2.1 %reshape.53 = bf16[1024,512]{1,0:T(8,128)(2,1)} reshape(bf16[32,32,8,64]{3,2,1,0:T(8,128)(2,1)S(1)} %copy.28) | data formatting | bytes 2097152 | tf_op jit(solution)/shard_map/reshape | solution.py:163
  97.8 1.9 fusion.4
  99.6 0.8 fusion.7
  100.4 0.0 copy-done.1
  100.4 0.0 copy-start.2
  100.4 0.0 copy-start.3
  100.4 1.8 fusion.1
  102.3 0.0 copy-done.2
  102.3 1.4 convolution_bitcast_fusion
  103.7 0.0 all-reduce.2.cloned.1.call-update
  103.7 0.7 constant_dynamic-slice_fusion
  104.4 3.4 %all-to-all-start = ((f32[8,2,8,256]{3,2,1,0:T(8,128)}), f32[8,2,8,256]{3,2,1,0:T(8,128)S(1)}, u32[]{:S(2)}, u32[]{:S(2)}) async-start(f32[8,2,8,256]{3,2,1,0:T(8,128)} %bitcast.14), calls=%async_computation | async-start | bytes 262144 | tf_op jit(solution)/shard_map/all_to_all | solution.py:173
  108.4 0.0 copy-done.3
  108.4 1.3 convolution_multiply_fusion.1
  109.7 32.8 %psum.14 = f32[]{:T(128)} all-reduce(f32[]{:T(128)S(6)} %mul_shard_map.3), channel_id=1, replica_groups=mesh['parts'=2,'blk'=16] {'blk'}, use_global_device_ids=true, to_apply=%region_1.2 | all-reduce | flops 1 | bytes 8 | tf_op jit(solution)/shard_map/psum | solution.py:175
  143.1 46.6 %all-reduce.2.cloned.1.call-done = f32[128,256]{0,1:T(8,128)} async-done(((f32[128,256]{0,1:T(8,128)}), f32[128,256]{0,1:T(8,128)}) %all-reduce.2.cloned.1.call-update) | async-done | bytes 131088 | tf_op jit(solution)/shard_map/psum | solution.py:175
  189.8 1.7 copy.30
  191.4 0.0 all-to-all-done
  191.4 0.7 copy_bitcast_fusion.1
  (6 shorter events, 0.0 us)
Async XLA Ops:
  7.2 43.7 %copy-start = (bf16[128,256]{1,0:T(8,128)(2,1)S(1)}, bf16[128,256]{1,0:T(8,128)(2,1)}, u32[]{:S(2)}) copy-start(bf16[128,256]{1,0:T(8,128)(2,1)} %param.9) | copy-start | bytes 196612
  7.2 43.7 %all-gather.5.cloned.1.call-start = ((), (), s32[]{:S(2)}) async-start(), calls=%async_computation.1 | async-start | bytes 1114112 | tf_op jit(solution)/shard_map/all_gather | solution.py:145
  7.9 82.0 %all-gather.7.cloned.1.call-start = ((), (), s32[]{:S(2)}) async-start(), calls=%async_computation.2 | async-start | bytes 1114112 | tf_op jit(solution)/shard_map/all_gather | solution.py:147
  8.7 181.1 %all-reduce.2.cloned.1.call-start = ((), (), s32[]{:S(2)}) async-start(), calls=%async_computation.3 | async-start | bytes 262144 | tf_op jit(solution)/shard_map/psum | solution.py:175
  8.7 6.5 %copy-start.6 = (s32[256,1]{0,1:T(1,128)S(1)}, s32[256,1]{0,1:T(1,128)}, u32[]{:S(2)}) copy-start(s32[256,1]{0,1:T(1,128)} %param.13) | copy-start | bytes 3076
  8.8 6.5 %copy-start.7 = (s32[256]{0:T(256)S(1)}, s32[256]{0:T(256)}, u32[]{:S(2)}) copy-start(s32[256]{0:T(256)} %param.14) | copy-start | bytes 3076
  8.8 6.5 %copy-start.8 = (s32[256]{0:T(256)S(1)}, s32[256]{0:T(256)}, u32[]{:S(2)}) copy-start(s32[256]{0:T(256)} %param.15) | copy-start | bytes 3076
  60.4 33.2 %copy-start.5 = (f32[256]{0:T(256)S(1)}, f32[256]{0:T(256)}, u32[]{:S(2)}) copy-start(f32[256]{0:T(256)} %param.12) | copy-start | bytes 3076
  89.9 4.4 %copy-start.4 = (bf16[32,64,256]{2,1,0:T(8,128)(2,1)S(1)}, bf16[32,64,256]{2,1,0:T(8,128)(2,1)}, u32[]{:S(2)}) copy-start(bf16[32,64,256]{2,1,0:T(8,128)(2,1)} %all-gather.7.cloned.1.call-done) | copy-start | bytes 3145732
  97.8 2.7 %copy-start.1 = (f32[4096,256]{1,0:T(8,128)S(1)}, f32[4096,256]{1,0:T(8,128)}, u32[]{:S(2)}) copy-start(f32[4096,256]{1,0:T(8,128)} %get-tuple-element.23) | copy-start | bytes 12582916
  100.4 1.8 copy-start.2
  100.4 8.0 %copy-start.3 = (bf16[1024,512]{1,0:T(8,128)(2,1)S(1)}, bf16[1024,512]{1,0:T(8,128)(2,1)}, u32[]{:S(2)}) copy-start(bf16[1024,512]{1,0:T(8,128)(2,1)} %reshape.53) | copy-start | bytes 3145732
  104.4 87.0 %all-to-all-start = ((f32[8,2,8,256]{3,2,1,0:T(8,128)}), f32[8,2,8,256]{3,2,1,0:T(8,128)S(1)}, u32[]{:S(2)}, u32[]{:S(2)}) async-start(f32[8,2,8,256]{3,2,1,0:T(8,128)} %bitcast.14), calls=%async_computation | async-start | bytes 262144 | tf_op jit(solution)/shard_map/all_to_all | solution.py:173
Sparse Core Ops, SparseCore 0:
  10.2 40.6 all-gather.4
  53.0 36.8 all-gather.6
  103.8 85.8 all-reduce.1

commit v2 on v1

--- a/solution.py
+++ b/solution.py
@@ -1,6 +1,8 @@
 import jax
 import jax.numpy as jnp
 from jax import lax
+from jax.experimental import pallas as pl
+from jax.experimental.pallas import tpu as pltpu
 from jax.sharding import PartitionSpec as P
 
 
@@ -128,6 +130,197 @@
     return (residual, loss, grad_first, grad_second)
 
 
+VMEM = pl.BlockSpec(memory_space=pltpu.VMEM)
+MESH = pl.DeviceIdType.MESH
+
+
+def greet(partners):
+    barrier = pltpu.get_barrier_semaphore()
+    for other in partners:
+        pl.semaphore_signal(barrier, inc=1, device_id={"blk": other}, device_id_type=MESH)
+    pl.semaphore_wait(barrier, len(partners))
+
+
+def gather_kernel(n, count, *refs):
+    ins, outs = refs[:count], refs[count : 2 * count]
+    send_sem, recv_sem, local_sem = refs[2 * count :]
+    me = lax.axis_index("blk")
+    depth = n // 4
+    z, x, core = me // 4, (me // 2) % 2, me % 2
+
+    def at(zz, xx, cc):
+        return zz * 4 + xx * 2 + cc
+
+    x_peer, core_peer = at(z, 1 - x, core), at(z, x, 1 - core)
+    z_peers = [at((z + d) % depth, x, core) for d in range(1, depth)]
+    greet([x_peer, core_peer] + z_peers)
+
+    def copy(arr, source, block, peer, kind):
+        return pltpu.make_async_remote_copy(
+            src_ref=source,
+            dst_ref=outs[arr].at[block],
+            send_sem=send_sem.at[arr, block, kind],
+            recv_sem=recv_sem.at[arr, block],
+            device_id={"blk": peer},
+            device_id_type=MESH,
+        )
+
+    started = []
+
+    def send(arr, block, peer, kind, source=None):
+        item = copy(arr, outs[arr].at[block] if source is None else source, block, peer, kind)
+        item.start()
+        started.append(item)
+
+    def arrived(arr, block):
+        copy(arr, outs[arr].at[block], block, core_peer, 0).wait_recv()
+
+    own = []
+    for arr in range(count):
+        for k, peer in enumerate(z_peers):
+            send(arr, me, peer, 2 + k, ins[arr])
+        send(arr, me, x_peer, 0, ins[arr])
+        send(arr, me, core_peer, 1, ins[arr])
+        item = pltpu.make_async_copy(ins[arr], outs[arr].at[me], local_sem.at[arr])
+        item.start()
+        own.append(item)
+    for arr in range(count):
+        arrived(arr, x_peer)
+        send(arr, x_peer, core_peer, 1)
+        for block in z_peers:
+            arrived(arr, block)
+            send(arr, block, x_peer, 0)
+            send(arr, block, core_peer, 1)
+    for arr in range(count):
+        for d in range(1, depth):
+            block = at((z + d) % depth, 1 - x, core)
+            arrived(arr, block)
+            send(arr, block, core_peer, 1)
+    for arr in range(count):
+        for d in range(depth):
+            for xx in range(2):
+                arrived(arr, at((z + d) % depth, xx, 1 - core))
+        own[arr].wait()
+    for item in started:
+        item.wait_send()
+
+
+def gather_all(n, arrays):
+    count = len(arrays)
+    return pl.pallas_call(
+        lambda *refs: gather_kernel(n, count, *refs),
+        out_shape=[jax.ShapeDtypeStruct((n,) + a.shape, a.dtype) for a in arrays],
+        in_specs=[VMEM] * count,
+        out_specs=[VMEM] * count,
+        scratch_shapes=[
+            pltpu.SemaphoreType.DMA((count, n, 1 + n // 4)),
+            pltpu.SemaphoreType.DMA((count, n)),
+            pltpu.SemaphoreType.DMA((count,)),
+        ],
+        compiler_params=pltpu.CompilerParams(
+            collective_id=0, has_side_effects=True, vmem_limit_bytes=32 * 2**20
+        ),
+        name="gather_all",
+    )(*arrays)
+
+
+def finish_kernel(n, term, square, mine, first, loss, resid, land, loss_land, total, *sems):
+    send_t, recv_t, send_l, recv_l, send_r, recv_r, send_g, recv_g = sems
+    me = lax.axis_index("blk")
+    half = n // 2
+    side, spot = me // half, me % half
+    rows = mine.shape[2]
+    others = [(me + k) % n for k in range(1, n)]
+    greet(others)
+
+    def copy(src, dst, send_sem, recv_sem, peer):
+        return pltpu.make_async_remote_copy(
+            src_ref=src,
+            dst_ref=dst,
+            send_sem=send_sem,
+            recv_sem=recv_sem,
+            device_id={"blk": peer},
+            device_id_type=MESH,
+        )
+
+    started = []
+    for k, peer in enumerate(others):
+        started.append(copy(term.at[peer], land.at[me], send_t.at[k], recv_t.at[me], peer))
+        started.append(copy(square, loss_land.at[me], send_l.at[k], recv_l.at[me], peer))
+    for k in range(1, half):
+        near = (spot + k) % half
+        started.append(
+            copy(
+                mine.at[near],
+                resid.at[:, pl.ds(pl.multiple_of(spot * rows, 8), rows), :],
+                send_r.at[k],
+                recv_r.at[spot],
+                side * half + near,
+            )
+        )
+    for item in started:
+        item.start()
+    land[me] = term[me]
+    loss_land[me] = square[...]
+    resid[:, pl.ds(pl.multiple_of(spot * rows, 8), rows), :] = mine[spot]
+    for peer in others:
+        copy(term.at[me], land.at[peer], send_t.at[0], recv_t.at[peer], peer).wait_recv()
+    added = land[0]
+    for d in range(1, n):
+        added = added + land[d]
+    total[...] = added
+    final = []
+    for k, peer in enumerate(others):
+        item = copy(total, first.at[me], send_g.at[k], recv_g.at[me], peer)
+        item.start()
+        final.append(item)
+    first[me] = added
+    for peer in others:
+        copy(square, loss_land.at[peer], send_l.at[0], recv_l.at[peer], peer).wait_recv()
+    squares = loss_land[0]
+    for d in range(1, n):
+        squares = squares + loss_land[d]
+    loss[...] = squares
+    for k in range(1, half):
+        near = (spot + k) % half
+        copy(
+            mine.at[near],
+            resid.at[:, pl.ds(pl.multiple_of(near * rows, 8), rows), :],
+            send_r.at[k],
+            recv_r.at[near],
+            side * half + near,
+        ).wait_recv()
+    for peer in others:
+        copy(total, first.at[peer], send_g.at[0], recv_g.at[peer], peer).wait_recv()
+    for item in started + final:
+        item.wait_send()
+
+
+def finish(n, term, square, mine):
+    half, blk_dev, rows, columns = mine.shape
+    dma = pltpu.SemaphoreType.DMA
+    return pl.pallas_call(
+        lambda *refs: finish_kernel(n, *refs),
+        out_shape=[
+            jax.ShapeDtypeStruct(term.shape, jnp.float32),
+            jax.ShapeDtypeStruct(square.shape, jnp.float32),
+            jax.ShapeDtypeStruct((blk_dev, half * rows, columns), jnp.float32),
+        ],
+        in_specs=[VMEM] * 3,
+        out_specs=[VMEM] * 3,
+        scratch_shapes=[
+            pltpu.VMEM(term.shape, jnp.float32),
+            pltpu.VMEM((n,) + square.shape, jnp.float32),
+            pltpu.VMEM(term.shape[1:], jnp.float32),
+        ]
+        + [dma((n,))] * 8,
+        compiler_params=pltpu.CompilerParams(
+            collective_id=1, has_side_effects=True, vmem_limit_bytes=32 * 2**20
+        ),
+        name="finish",
+    )(term, square, mine)
+
+
 def fast_local(features, w_first, w_second, panel, energies, pair_dest, pair_row, pair_col):
     n_dev = lax.axis_size("blk")
     me = lax.axis_index("blk")
@@ -142,19 +335,29 @@
     spot = me % half
     f32 = jnp.float32
     gid = pair_col * blocks + pair_dest[:, 0] * blk_dev + pair_row
-    feats = lax.all_gather(features, "blk", axis=0, tiled=True)
-    gids = lax.all_gather(gid, "blk", axis=0, tiled=False)
-    coeffs = lax.all_gather(panel, "blk", axis=0, tiled=True)
+    ids = jnp.broadcast_to(gid.reshape(1, pairs), (8, pairs))
+    feats, gids, coeffs = gather_all(
+        n_dev, (features, ids, panel.reshape(blk_dev * orbitals, columns))
+    )
+    feats = feats.reshape(n_dev * pairs, width)
+    gids = gids[:, 0, :]
+    coeffs = coeffs.reshape(blocks, orbitals, columns)
     pre = jnp.dot(feats, w_first, preferred_element_type=f32)
     sig = jax.nn.sigmoid(pre)
     hidden = (pre * sig).astype(jnp.bfloat16)
     onehot = (gids[:, None, :] == jnp.arange(groups, dtype=jnp.int32)[None, :, None]).astype(jnp.bfloat16)
     summed = jnp.einsum("dgp,dpk->dgk", onehot, hidden.reshape(n_dev, pairs, hid), preferred_element_type=f32)
     summed = summed.astype(jnp.bfloat16).reshape(n_dev * groups, hid)
-    w_sides = w_second.reshape(hid, 2, orbitals * orbitals)
-    w_part = lax.dynamic_slice_in_dim(w_sides, spot * a_count * orbitals, a_count * orbitals, 2)
-    w_own = lax.dynamic_index_in_dim(w_part, side, 1, keepdims=False)
-    mats = jnp.dot(summed, w_part.reshape(hid, -1), preferred_element_type=f32) / orbitals
+    span = a_count * orbitals
+    w_part = jnp.concatenate(
+        [
+            lax.dynamic_slice_in_dim(w_second, part * orbitals * orbitals + spot * span, span, 1)
+            for part in range(2)
+        ],
+        axis=1,
+    )
+    w_own = lax.dynamic_slice_in_dim(w_second, me * span, span, 1)
+    mats = jnp.dot(summed, w_part, preferred_element_type=f32) / orbitals
     mats = mats.astype(jnp.bfloat16).reshape(blocks, blocks, 2, a_count, orbitals)
     both = jnp.einsum("crhab,cbp->hrap", mats, coeffs, preferred_element_type=f32)
     resid = both[0] - both[1] * energies
@@ -169,11 +372,10 @@
     term_first = jnp.dot(feats.T, d_pre, preferred_element_type=f32)
     mine = lax.dynamic_slice_in_dim(resid, side * (blocks // 2), blocks // 2, 0)
     mine = mine.reshape(half, blk_dev, a_count, columns)
-    sides = [list(range(half)), list(range(half, n_dev))]
-    got = lax.all_to_all(mine, "blk", 0, 0, axis_index_groups=sides, tiled=True)
-    residual = got.transpose(1, 0, 2, 3).reshape(blk_dev, orbitals, columns)
-    grad_first, square_sum = lax.psum((term_first, 0.5 * jnp.sum(resid * resid)), "blk")
-    loss = (square_sum / (blocks * orbitals * columns)).reshape(1)
+    square = jnp.full((8, 128), 0.5 * jnp.sum(resid * resid), f32)
+    first, loss_sum, residual = finish(n_dev, term_first.reshape(n_dev, width // n_dev, hid), square, mine)
+    grad_first = first.reshape(width, hid)
+    loss = loss_sum[0, :1] / (blocks * orbitals * columns)
     return (residual, loss, grad_first, grad_second)
 
 
@@ -190,4 +392,4 @@
     )
     out_specs = (P(("parts", "blk"), None, None), P("parts"), P("parts", None), P("parts", "blk"))
     return jax.shard_map(
-        fast_local if mesh.shape["blk"] <= 32 else local, mesh=mesh, in_specs=in_specs, out_specs=out_specs, check_vma=False)
+        fast_local if mesh.shape["blk"] == 16 else local, mesh=mesh, in_specs=in_specs, out_specs=out_specs, check_vma=False)

time: 201 us -> 81 us (0.40)
  waiting for transfers between devices: 89 us -> 0 us
  blocking collectives: 55.9 us -> 0 us
  Pallas kernels: 0 us -> 42.2 us
  between operations: 16.4 us -> 3.29 us
  starting transfers between devices: 3.49 us -> 0 us
    psum x1 -> x0, waiting for transfers between devices: 46.6 us -> none  [fast_local(): lax.psum((term_first, 0.5 * jnp.sum(resid * resid)), 'blk')]
    pallas_call x0 -> x2, Pallas kernels: none -> 42.2 us  [the longest x1 25.7 us: gather_all(): pl.pallas_call(lambda *refs: gather_kernel(n, count, *refs), out_shape=[j...]
    all_gather x2 -> x0, waiting for transfers between devices: 40.9 us -> none  [the longest x1 29.5 us: fast_local(): coeffs = lax.all_gather(panel, 'blk', axis=0, tiled=True)]
    psum x1 -> x0, blocking collectives: 32.8 us -> none  [fast_local(): lax.psum((term_first, 0.5 * jnp.sum(resid * resid)), 'blk')]
    all_gather x1 -> x0, blocking collectives: 23.1 us -> none  [fast_local(): gids = lax.all_gather(gid, 'blk', axis=0, tiled=False)]
    unnamed x21 -> x19, local copies, waits for them, and re-layouts: 8.14 us -> 3.03 us
    all_to_all x1 -> x0, starting transfers between devices: 3.37 us -> none  [fast_local(): got = lax.all_to_all(mine, 'blk', 0, 0, axis_index_groups=sides, tiled=True)]
    reshape x1, local copies, waits for them, and re-layouts: 4.08 us -> 6.42 us  [fast_local(): mats.astype(jnp.bfloat16).reshape(blocks, blocks, 2, a_count, orbitals)]
  transfers between devices with their start and end apart: 4 -> 0, of which waited for: 3 -> 0; matrix products, arithmetic and copies ran while one was open for 10% -> 0% of each run, Pallas kernels for 0% -> 0%
where the time goes in v2:
time: 81 us; the launch traced here: 80.6 us
  Pallas kernels  42.2 us (52%)
  local copies, waits for them, and re-layouts  15.5 us (19%)
  matrix products  15.5 us (19%)
  other arithmetic  4.05 us (5%)
  between operations  3.29 us (4%)
    pallas_call x1, Pallas kernels, gather_all(): pl.pallas_call(lambda *refs: gather_kernel(n, count, *refs), out_shape=[j...  25.7 us
    pallas_call x1, Pallas kernels, finish(): pl.pallas_call(lambda *refs: finish_kernel(n, *refs), out_shape=[jax.Shap...  16.5 us
    reshape x1, local copies, waits for them, and re-layouts, fast_local(): mats.astype(jnp.bfloat16).reshape(blocks, blocks, 2, a_count, orbitals)  6.42 us
    dot_general x1, matrix products, fast_local(): jnp.einsum('crhab,cbp->hrap', mats, coeffs, preferred_element_type=f32)  3.46 us
    dot_general x1, matrix products, fast_local(): pre = jnp.dot(feats, w_first, preferred_element_type=f32)  3.11 us
    unnamed x19, local copies, waits for them, and re-layouts  3.03 us
    dot_general x1, matrix products, fast_local(): jnp.dot(summed.T, d_mats, preferred_element_type=f32) / orbitals  2.78 us
    dot_general x1, matrix products, fast_local(): mats = jnp.dot(summed, w_part, preferred_element_type=f32) / orbitals  2.07 us

profile of v2, /device:TPU:0, one launch (start us, length us, event | category | flops | bytes accessed | tf_op | source)
XLA Modules:
  0.0 80.6 jit_solution(13831137309220597147)
XLA Ops:
  0.6 0.0 copy-start
  0.7 0.7 broadcast_multiply_fusion
  1.4 0.7 add_add_fusion
  2.1 1.8 %constant_dynamic-slice_fusion.2 = (bf16[256,512]{1,0:T(8,128)(2,1)}, bf16[256,512]{1,0:T(8,128)(2,1)}) fusion(bf16[256,8192]{1,0:T(8,128)(2,1)} %param.10, s32[]{:T(128)S(6)} %select_n.35, s32[]{:T(128)S(6)} %select_n.36), kind=kLoop, calls=%fused_computation.36 | loop fusion | bytes 1048584 | tf_op jit(solution)/shard_map/dynamic_slice | solution.py:354
  3.9 0.0 copy-start.1
  3.9 0.8 %copy-done.1 = bf16[256,128]{1,0:T(8,128)(2,1)S(1)} copy-done((bf16[256,128]{1,0:T(8,128)(2,1)S(1)}, bf16[256,128]{1,0:T(8,128)(2,1)}, u32[]{:S(2)}) %copy-start.1) | copy-done | bytes 65560
  4.8 0.0 copy-start.2
  4.8 0.8 %copy-done.2 = bf16[2,64,256]{2,1,0:T(8,128)(2,1)S(1)} copy-done((bf16[2,64,256]{2,1,0:T(8,128)(2,1)S(1)}, bf16[2,64,256]{2,1,0:T(8,128)(2,1)}, u32[]{:S(2)}) %copy-start.2) | copy-done | bytes 65560
  5.6 25.7 %gather_all.1 = (bf16[16,256,128]{2,1,0:T(8,128)(2,1)S(1)}, s32[16,8,256]{2,1,0:T(8,128)S(1)}, bf16[16,128,256]{2,1,0:T(8,128)(2,1)S(1)}) custom-call(bf16[256,128]{1,0:T(8,128)(2,1)S(1)} %copy-done.1, s32[8,256]{1,0:T(8,128)S(1)} %broadcast_in_dim.4.refs_1_, bf16[128,256]{1,0:T(8,128)(2,1)S(1)} %bitcast.72), custom_call_target="tpu_custom_call" | custom-call | tf_op jit(solution)/shard_map/gather_all/pallas_call | solution.py:210
  31.3 0.5 copy.15
  31.9 0.0 copy-done
  31.9 0.0 copy-start.5
  31.9 0.0 copy-start.6
  31.9 3.1 %multiply_convert_fusion.1 = (bf16[4096,256]{1,0:T(8,128)(2,1)S(1)}, f32[4096,256]{1,0:T(8,128)}) fusion(bf16[4096,128]{1,0:T(8,128)(2,1)S(1)} %bitcast.67, bf16[128,256]{1,0:T(8,128)(2,1)S(1)} %copy-done), kind=kOutput, calls=%fused_computation.6 | convolution fusion | flops 273678336 | bytes 7405568 | tf_op jit(solution)/shard_map/dot_general | solution.py:345
  35.0 0.4 convolution_convert_fusion
  35.4 0.0 copy-start.4
  35.4 0.0 copy-done.5
  35.4 0.0 copy-done.6
  35.5 2.1 %multiply_convert_fusion = bf16[1024,1024]{1,0:T(8,128)(2,1)} fusion(bf16[1024,256]{1,0:T(8,128)(2,1)S(1)} %bitcast.74, bf16[256,512]{1,0:T(8,128)(2,1)S(1)} %copy-done.6, bf16[256,512]{1,0:T(8,128)(2,1)S(1)} %copy-done.5), kind=kOutput, calls=%fused_computation.5 | convolution fusion | flops 540016640 | bytes 3145728 | tf_op jit(solution)/shard_map/dot_general | solution.py:360
  37.5 0.0 copy-done.4
  37.5 6.4 %reshape.56 = bf16[32,32,2,8,64]{4,3,2,1,0:T(8,128)(2,1)} reshape(bf16[1024,1024]{1,0:T(8,128)(2,1)} %multiply_convert_fusion) | data formatting | bytes 4194304 | tf_op jit(solution)/shard_map/reshape | solution.py:361
  43.9 0.0 copy-start.7
  43.9 3.5 %fusion.7 = f32[2,32,8,256]{3,1,2,0:T(8,128)S(1)} fusion(bf16[32,64,256,1,1]{2,1,0,4,3:T(8,128)(2,1)S(1)} %bitcast.68, bf16[32,32,2,8,64]{4,3,2,1,0:T(8,128)(2,1)} %reshape.56), kind=kOutput, calls=%fused_computation.15 | convolution fusion | flops 536870912 | bytes 3670016 | tf_op jit(solution)/shard_map/crhab,cbp->hrap/dot_general | solution.py:362
  47.4 0.0 copy-done.7
  47.4 0.7 multiply_reduce_fusion
  48.8 0.1 copy.18
  48.9 0.7 convert_bitcast_fusion
  49.6 1.0 %copy.17 = bf16[32,32,8,64]{3,2,1,0:T(8,128)(2,1)S(1)} copy(bf16[32,32,8,64]{3,1,2,0:T(8,128)(2,1)S(1)} %convert_bitcast_fusion) | data formatting | bytes 2097152 | tf_op jit(solution)/shard_map/convert_element_type | solution.py:366
  50.6 2.1 %reshape.57 = bf16[1024,512]{1,0:T(8,128)(2,1)} reshape(bf16[32,32,8,64]{3,2,1,0:T(8,128)(2,1)S(1)} %copy.17) | data formatting | bytes 2097152 | tf_op jit(solution)/shard_map/reshape | solution.py:366
  52.7 0.0 copy-start.3
  52.7 2.8 %convolution_multiply_fusion.1 = f32[256,512]{1,0:T(8,128)} fusion(bf16[1024,256]{1,0:T(8,128)(2,1)} %bitcast.75, bf16[1024,512]{1,0:T(8,128)(2,1)} %reshape.57), kind=kOutput, calls=%fused_computation.14 | convolution fusion | flops 268566528 | bytes 2097152 | tf_op jit(solution)/shard_map/dot_general | solution.py:367
  55.5 1.7 %fusion.6 = bf16[1024,256]{1,0:T(8,128)(2,1)S(1)} fusion(bf16[1024,512]{1,0:T(8,128)(2,1)} %reshape.57, bf16[256,8192]{1,0:T(8,128)(2,1)} %param.10, s32[]{:T(128)S(6)} %select_n.38), kind=kOutput, calls=%fused_computation.12 | convolution fusion | flops 268959744 | bytes 1835012 | tf_op jit(solution)/shard_map/dot_general | solution.py:368
  57.2 0.8 fusion.11
  58.0 0.0 copy-done.3
  58.0 2.0 %fusion.1 = bf16[4096,256]{1,0:T(8,128)(2,1)S(1)} fusion(f32[16,256,256]{2,1,0:T(8,128)S(1)} %fusion.11, f32[4096,256]{1,0:T(8,128)S(1)} %copy-done.3), kind=kLoop, calls=%fused_computation.2 | loop fusion | flops 9437184 | bytes 10485760 | tf_op jit(solution)/shard_map/convert_element_type | solution.py:371
  60.0 0.5 fusion.4.refs_0_
  60.5 16.5 %finish.1 = (f32[16,8,256]{2,1,0:T(8,128)S(1)}, f32[8,128]{1,0:T(8,128)S(1)}, f32[2,64,256]{2,1,0:T(8,128)S(1)}) custom-call(f32[16,8,256]{2,1,0:T(8,128)S(1)} %fusion.4.refs_0_, f32[8,128]{1,0:T(8,128)S(1)} %broadcast_in_dim.5.refs_1_, f32[8,2,8,256]{3,2,1,0:T(8,128)S(1)} %bitcast.70), custom_call_target="tpu_custom_call" | custom-call | tf_op jit(solution)/shard_map/finish/pallas_call | solution.py:302
  77.0 0.5 slice.15
  78.1 0.7 copy.31
  78.8 0.7 copy.32
  (5 shorter events, 0.0 us)
Async XLA Ops:
  0.6 31.2 %copy-start = (bf16[128,256]{1,0:T(8,128)(2,1)S(1)}, bf16[128,256]{1,0:T(8,128)(2,1)}, u32[]{:S(2)}) copy-start(bf16[128,256]{1,0:T(8,128)(2,1)} %param.9) | copy-start | bytes 196612
  3.9 0.8 %copy-start.1 = (bf16[256,128]{1,0:T(8,128)(2,1)S(1)}, bf16[256,128]{1,0:T(8,128)(2,1)}, u32[]{:S(2)}) copy-start(bf16[256,128]{1,0:T(8,128)(2,1)} %refs_0_.1) | copy-start | bytes 196612
  4.8 0.8 %copy-start.2 = (bf16[2,64,256]{2,1,0:T(8,128)(2,1)S(1)}, bf16[2,64,256]{2,1,0:T(8,128)(2,1)}, u32[]{:S(2)}) copy-start(bf16[2,64,256]{2,1,0:T(8,128)(2,1)} %param.11) | copy-start | bytes 196612
  31.9 3.6 %copy-start.5 = (bf16[256,512]{1,0:T(8,128)(2,1)S(1)}, bf16[256,512]{1,0:T(8,128)(2,1)}, u32[]{:S(2)}) copy-start(bf16[256,512]{1,0:T(8,128)(2,1)} %get-tuple-element.18) | copy-start | bytes 786436
  31.9 3.6 %copy-start.6 = (bf16[256,512]{1,0:T(8,128)(2,1)S(1)}, bf16[256,512]{1,0:T(8,128)(2,1)}, u32[]{:S(2)}) copy-start(bf16[256,512]{1,0:T(8,128)(2,1)} %get-tuple-element.19) | copy-start | bytes 786436
  35.4 2.1 %copy-start.4 = (bf16[16,64,256]{2,1,0:T(8,128)(2,1)}, bf16[16,64,256]{2,1,0:T(8,128)(2,1)S(1)}, u32[]{:S(2)}) copy-start(bf16[16,64,256]{2,1,0:T(8,128)(2,1)S(1)} %convolution_convert_fusion) | copy-start | bytes 1572868
  43.9 3.5 %copy-start.7 = (f32[256]{0:T(256)S(1)}, f32[256]{0:T(256)}, u32[]{:S(2)}) copy-start(f32[256]{0:T(256)} %param.12) | copy-start | bytes 3076
  52.7 5.3 %copy-start.3 = (f32[4096,256]{1,0:T(8,128)S(1)}, f32[4096,256]{1,0:T(8,128)}, u32[]{:S(2)}) copy-start(f32[4096,256]{1,0:T(8,128)} %get-tuple-element.21) | copy-start | bytes 12582916

commit v3 on v2

--- a/solution.py
+++ b/solution.py
@@ -152,8 +152,7 @@
         return zz * 4 + xx * 2 + cc
 
     x_peer, core_peer = at(z, 1 - x, core), at(z, x, 1 - core)
-    z_peers = [at((z + d) % depth, x, core) for d in range(1, depth)]
-    greet([x_peer, core_peer] + z_peers)
+    greet([x_peer, core_peer] + [at((z + d) % depth, x, core) for d in range(1, depth)])
 
     def copy(arr, source, block, peer, kind):
         return pltpu.make_async_remote_copy(
@@ -165,44 +164,73 @@
             device_id_type=MESH,
         )
 
-    started = []
-
-    def send(arr, block, peer, kind, source=None):
-        item = copy(arr, outs[arr].at[block] if source is None else source, block, peer, kind)
-        item.start()
-        started.append(item)
-
     def arrived(arr, block):
         copy(arr, outs[arr].at[block], block, core_peer, 0).wait_recv()
 
+    def spread(arr, zz, act, up, down, source=None):
+        block = at(zz, x, core)
+        source = outs[arr].at[block] if source is None else source
+
+        if up:
+
+            @pl.when(z < depth - 1)
+            def go_up():
+                act(copy(arr, source, block, at(z + 1, x, core), 2))
+
+        if down:
+
+            @pl.when(z > 0)
+            def go_down():
+                act(copy(arr, source, block, at(z - 1, x, core), 3))
+
+        act(copy(arr, source, block, x_peer, 0))
+        act(copy(arr, source, block, core_peer, 1))
+
+    def each_dist(fn):
+        for dist in range(1, depth):
+
+            @pl.when(z >= dist)
+            def below(dist=dist):
+                fn(z - dist, True, False)
+
+            @pl.when(z + dist < depth)
+            def above(dist=dist):
+                fn(z + dist, False, True)
+
+    begin = lambda item: item.start()
+    ended = lambda item: item.wait_send()
     own = []
     for arr in range(count):
-        for k, peer in enumerate(z_peers):
-            send(arr, me, peer, 2 + k, ins[arr])
-        send(arr, me, x_peer, 0, ins[arr])
-        send(arr, me, core_peer, 1, ins[arr])
+        spread(arr, z, begin, True, True, ins[arr])
         item = pltpu.make_async_copy(ins[arr], outs[arr].at[me], local_sem.at[arr])
         item.start()
         own.append(item)
+
     for arr in range(count):
-        arrived(arr, x_peer)
-        send(arr, x_peer, core_peer, 1)
-        for block in z_peers:
+
+        def relay(zz, up, down):
+            arrived(arr, at(zz, x, core))
+            spread(arr, zz, begin, up, down)
+
+        each_dist(relay)
+
+        def across(zz, up=False, down=False):
+            block = at(zz, 1 - x, core)
             arrived(arr, block)
-            send(arr, block, x_peer, 0)
-            send(arr, block, core_peer, 1)
+            begin(copy(arr, outs[arr].at[block], block, core_peer, 1))
+
+        across(z)
+        each_dist(across)
     for arr in range(count):
-        for d in range(1, depth):
-            block = at((z + d) % depth, 1 - x, core)
-            arrived(arr, block)
-            send(arr, block, core_peer, 1)
-    for arr in range(count):
-        for d in range(depth):
+        for zz in range(depth):
             for xx in range(2):
-                arrived(arr, at((z + d) % depth, xx, 1 - core))
+                arrived(arr, at(zz, xx, 1 - core))
         own[arr].wait()
-    for item in started:
-        item.wait_send()
+        spread(arr, z, ended, True, True, ins[arr])
+        each_dist(lambda zz, up, down: spread(arr, zz, ended, up, down))
+        for zz in range(depth):
+            block = at(zz, 1 - x, core)
+            ended(copy(arr, outs[arr].at[block], block, core_peer, 1))
 
 
 def gather_all(n, arrays):
@@ -213,7 +241,7 @@
         in_specs=[VMEM] * count,
         out_specs=[VMEM] * count,
         scratch_shapes=[
-            pltpu.SemaphoreType.DMA((count, n, 1 + n // 4)),
+            pltpu.SemaphoreType.DMA((count, n, 4)),
             pltpu.SemaphoreType.DMA((count, n)),
             pltpu.SemaphoreType.DMA((count,)),
         ],
@@ -321,6 +349,127 @@
     )(term, square, mine)
 
 
+def swap_halves(top, bottom):
+    low = lax.broadcasted_iota(jnp.int32, top.shape, 1) < 64
+    return (
+        jnp.where(low, top, pltpu.roll(bottom, 64, 1)),
+        jnp.where(low, pltpu.roll(top, 64, 1), bottom),
+    )
+
+
+def compute_kernel(
+    n, blocks, a_count, feats, ids, coeffs, w_first, w_part, w_own, energies, grad_scale,
+    second_out, first_out, resid_out, square_out, slope, summed, mats, d_mats, d_sum
+):
+    f32, bf16 = jnp.float32, jnp.bfloat16
+    orbitals = 64
+    groups = 2 * blocks
+    lanes = 2 * orbitals
+    pairs = feats.shape[1]
+
+    def onehot(b):
+        rows = lax.broadcasted_iota(jnp.int32, (groups, pairs), 0)
+        return jnp.where(rows == ids[b][0:1, :], 1.0, 0.0).astype(bf16)
+
+    def predict_block(b, carry):
+        pre = jnp.dot(feats[b], w_first[...], preferred_element_type=f32)
+        sig = 1.0 / (1.0 + jnp.exp(-pre))
+        slope[b] = sig * (1.0 + pre * (1.0 - sig))
+        hidden = (pre * sig).astype(bf16)
+        total = jnp.dot(onehot(b), hidden, preferred_element_type=f32).astype(bf16)
+        summed[pl.ds(pl.multiple_of(b * groups, groups), groups), :] = total
+        made = jnp.dot(total, w_part[...], preferred_element_type=f32) / orbitals
+        where_b = pl.ds(pl.multiple_of(b * lanes, lanes), lanes)
+        for pair in range(a_count):
+            slab = made[:, pair * lanes : (pair + 1) * lanes]
+            even, odd = swap_halves(slab[:blocks], slab[blocks:])
+            start = 2 * pair * blocks
+            mats[start : start + blocks, where_b] = even.astype(bf16)
+            mats[start + blocks : start + 2 * blocks, where_b] = odd.astype(bf16)
+        return carry
+
+    lax.fori_loop(0, n, predict_block, 0)
+    rows = a_count * blocks
+    h_part = jnp.dot(mats[:rows, :], coeffs[...], preferred_element_type=f32)
+    s_part = jnp.dot(mats[rows:, :], coeffs[...], preferred_element_type=f32)
+    resid = h_part - s_part * energies[...]
+    resid_out[...] = resid
+    square_out[...] = jnp.full(square_out.shape, 0.5 * jnp.sum(resid * resid), f32)
+    grad = (resid * grad_scale[...]).astype(bf16)
+
+    def back_block(b, carry):
+        where_b = pl.ds(pl.multiple_of(b * lanes, lanes), lanes)
+        got = lax.dot_general(
+            grad, coeffs[where_b, :], (((1,), (1,)), ((), ())), preferred_element_type=f32
+        )
+        for pair in range(a_count // 2):
+            start = 2 * pair * blocks
+            even, odd = swap_halves(
+                got[start : start + blocks], got[start + blocks : start + 2 * blocks]
+            )
+            cols = slice(pair * lanes, (pair + 1) * lanes)
+            base = pl.multiple_of(b * groups, groups)
+            d_mats[pl.ds(base, groups), cols] = jnp.concatenate([even, odd], axis=0).astype(bf16)
+        return carry
+
+    lax.fori_loop(0, n, back_block, 0)
+    second_out[...] = (
+        lax.dot_general(
+            summed[...], d_mats[...], (((0,), (0,)), ((), ())), preferred_element_type=f32
+        )
+        / orbitals
+    )
+    d_sum[...] = (
+        lax.dot_general(
+            d_mats[...], w_own[...], (((1,), (1,)), ((), ())), preferred_element_type=f32
+        )
+        / orbitals
+    ).astype(bf16)
+    first_out[...] = jnp.zeros(first_out.shape, f32)
+
+    def first_block(b, carry):
+        part = d_sum[pl.ds(pl.multiple_of(b * groups, groups), groups), :]
+        spread = lax.dot_general(
+            onehot(b), part, (((0,), (0,)), ((), ())), preferred_element_type=f32
+        )
+        d_pre = (spread * slope[b]).astype(bf16)
+        first_out[...] += lax.dot_general(
+            feats[b], d_pre, (((0,), (0,)), ((), ())), preferred_element_type=f32
+        )
+        return carry
+
+    lax.fori_loop(0, n, first_block, 0)
+
+
+def compute(n, blocks, a_count, *args):
+    feats, ids, coeffs, w_first, w_part, w_own = args[:6]
+    f32, bf16 = jnp.float32, jnp.bfloat16
+    width, hid = w_first.shape
+    pairs = feats.shape[1]
+    columns = coeffs.shape[1]
+    shape = jax.ShapeDtypeStruct
+    return pl.pallas_call(
+        lambda *refs: compute_kernel(n, blocks, a_count, *refs),
+        out_shape=[
+            shape((hid, w_own.shape[1]), f32),
+            shape((width, hid), f32),
+            shape((a_count * blocks, columns), f32),
+            shape((8, 128), f32),
+        ],
+        in_specs=[VMEM] * 8,
+        out_specs=[VMEM] * 4,
+        scratch_shapes=[
+            pltpu.VMEM((n, pairs, hid), f32),
+            pltpu.VMEM((blocks * blocks, hid), bf16),
+            pltpu.VMEM((2 * a_count * blocks, coeffs.shape[0]), bf16),
+            pltpu.VMEM((blocks * blocks, w_own.shape[1]), bf16),
+            pltpu.VMEM((blocks * blocks, hid), bf16),
+        ],
+        compiler_params=pltpu.CompilerParams(vmem_limit_bytes=48 * 2**20),
+        name="compute",
+    )(*args)
+
+
 def fast_local(features, w_first, w_second, panel, energies, pair_dest, pair_row, pair_col):
     n_dev = lax.axis_size("blk")
     me = lax.axis_index("blk")
@@ -328,7 +477,6 @@
     blk_dev, orbitals, columns = panel.shape
     hid = w_second.shape[0]
     blocks = blk_dev * n_dev
-    groups = blk_dev * blocks
     half = n_dev // 2
     a_count = orbitals // half
     side = me // half
@@ -339,15 +487,6 @@
     feats, gids, coeffs = gather_all(
         n_dev, (features, ids, panel.reshape(blk_dev * orbitals, columns))
     )
-    feats = feats.reshape(n_dev * pairs, width)
-    gids = gids[:, 0, :]
-    coeffs = coeffs.reshape(blocks, orbitals, columns)
-    pre = jnp.dot(feats, w_first, preferred_element_type=f32)
-    sig = jax.nn.sigmoid(pre)
-    hidden = (pre * sig).astype(jnp.bfloat16)
-    onehot = (gids[:, None, :] == jnp.arange(groups, dtype=jnp.int32)[None, :, None]).astype(jnp.bfloat16)
-    summed = jnp.einsum("dgp,dpk->dgk", onehot, hidden.reshape(n_dev, pairs, hid), preferred_element_type=f32)
-    summed = summed.astype(jnp.bfloat16).reshape(n_dev * groups, hid)
     span = a_count * orbitals
     w_part = jnp.concatenate(
         [
@@ -357,22 +496,23 @@
         axis=1,
     )
     w_own = lax.dynamic_slice_in_dim(w_second, me * span, span, 1)
-    mats = jnp.dot(summed, w_part, preferred_element_type=f32) / orbitals
-    mats = mats.astype(jnp.bfloat16).reshape(blocks, blocks, 2, a_count, orbitals)
-    both = jnp.einsum("crhab,cbp->hrap", mats, coeffs, preferred_element_type=f32)
-    resid = both[0] - both[1] * energies
-    grad = jnp.where(side == 0, resid / blocks, -(resid * energies) / blocks).astype(jnp.bfloat16)
-    d_mats = jnp.einsum("rap,cbp->crab", grad, coeffs, preferred_element_type=f32)
-    d_mats = d_mats.astype(jnp.bfloat16).reshape(blocks * blocks, a_count * orbitals)
-    grad_second = jnp.dot(summed.T, d_mats, preferred_element_type=f32) / orbitals
-    d_sum = lax.dot_general(d_mats, w_own, (((1,), (1,)), ((), ())), preferred_element_type=f32) / orbitals
-    d_sum = d_sum.astype(jnp.bfloat16).reshape(n_dev, groups, hid)
-    d_hidden = jnp.einsum("dgp,dgk->dpk", onehot, d_sum, preferred_element_type=f32).reshape(-1, hid)
-    d_pre = (d_hidden * sig * (1.0 + pre * (1.0 - sig))).astype(jnp.bfloat16)
-    term_first = jnp.dot(feats.T, d_pre, preferred_element_type=f32)
-    mine = lax.dynamic_slice_in_dim(resid, side * (blocks // 2), blocks // 2, 0)
-    mine = mine.reshape(half, blk_dev, a_count, columns)
-    square = jnp.full((8, 128), 0.5 * jnp.sum(resid * resid), f32)
+    grad_scale = jnp.where(side == 0, jnp.ones_like(energies), -energies) / blocks
+    grad_second, term_first, resid, square = compute(
+        n_dev,
+        blocks,
+        a_count,
+        feats,
+        gids,
+        coeffs.reshape(blocks * orbitals, columns),
+        w_first,
+        w_part,
+        w_own,
+        energies[None, :],
+        grad_scale[None, :],
+    )
+    resid = resid.reshape(a_count, blocks, columns)
+    mine = lax.dynamic_slice_in_dim(resid, side * (blocks // 2), blocks // 2, 1)
+    mine = mine.transpose(1, 0, 2).reshape(half, blk_dev, a_count, columns)
     first, loss_sum, residual = finish(n_dev, term_first.reshape(n_dev, width // n_dev, hid), square, mine)
     grad_first = first.reshape(width, hid)
     loss = loss_sum[0, :1] / (blocks * orbitals * columns)

time: 81 us -> 81.6 us (level)
  Pallas kernels: 42.2 us -> 70.3 us
  matrix products: 15.5 us -> 0 us
  local copies, waits for them, and re-layouts: 15.5 us -> 6.29 us
  other arithmetic: 4.05 us -> 2.13 us
    pallas_call x0 -> x1, Pallas kernels: none -> 22.4 us  [compute(): pl.pallas_call(lambda *refs: compute_kernel(n, blocks, a_count, *refs), o...]
    dot_general x9 -> x0, matrix products: 15.5 us -> none  [the longest x1 3.46 us: fast_local(): jnp.einsum('crhab,cbp->hrap', mats, coeffs, preferred_element_type=f32)]
    reshape x2 -> x0, local copies, waits for them, and re-layouts: 8.48 us -> none  [the longest x1 6.42 us: fast_local(): mats.astype(jnp.bfloat16).reshape(blocks, blocks, 2, a_count, orbitals)]
    pallas_call x1, Pallas kernels: 25.7 us -> 33.6 us  [gather_all(): pl.pallas_call(lambda *refs: gather_kernel(n, count, *refs), out_shape=[j...]
    pallas_call x1, Pallas kernels: 16.5 us -> 14.3 us  [finish(): pl.pallas_call(lambda *refs: finish_kernel(n, *refs), out_shape=[jax.Shap...]
    convert_element_type x1 -> x0, other arithmetic: 2 us -> none  [fast_local(): d_pre = (d_hidden * sig * (1.0 + pre * (1.0 - sig))).astype(jnp.bfloat16)]
    unnamed x19 -> x11, local copies, waits for them, and re-layouts: 3.03 us -> 4.58 us
    convert_element_type x1 -> x0, local copies, waits for them, and re-layouts: 0.99 us -> none  [fast_local(): d_mats.astype(jnp.bfloat16).reshape(blocks * blocks, a_count * orbitals)]
where the time goes in v3:
time: 81.6 us; the launch traced here: 81.2 us
  Pallas kernels  70.3 us (86%)
  local copies, waits for them, and re-layouts  6.29 us (8%)
  between operations  2.51 us (3%)
  other arithmetic  2.13 us (3%)
    pallas_call x1, Pallas kernels, gather_all(): pl.pallas_call(lambda *refs: gather_kernel(n, count, *refs), out_shape=[j...  33.6 us
    pallas_call x1, Pallas kernels, compute(): pl.pallas_call(lambda *refs: compute_kernel(n, blocks, a_count, *refs), o...  22.4 us
    pallas_call x1, Pallas kernels, finish(): pl.pallas_call(lambda *refs: finish_kernel(n, *refs), out_shape=[jax.Shap...  14.3 us
    unnamed x11, local copies, waits for them, and re-layouts  4.58 us

profile of v3, /device:TPU:0, one launch (start us, length us, event | category | flops | bytes accessed | tf_op | source)
XLA Modules:
  0.0 81.2 jit_solution(16784890843861219830)
XLA Ops:
  0.7 0.7 select_multiply_fusion
  1.4 0.7 broadcast_multiply_fusion
  2.0 0.7 add_add_fusion
  2.7 1.2 %constant_dynamic-slice_fusion.1 = (bf16[256,512]{1,0:T(8,128)(2,1)S(1)}, bf16[256,512]{1,0:T(8,128)(2,1)S(1)}, bf16[256,512]{1,0:T(8,128)(2,1)S(1)}) fusion(bf16[256,8192]{1,0:T(8,128)(2,1)} %param.10, s32[]{:T(128)S(6)} %select_n.34, s32[]{:T(128)S(6)} %select_n.32, s32[]{:T(128)S(6)} %select_n.33), kind=kLoop, calls=%fused_computation.3 | loop fusion | bytes 1572876 | tf_op jit(solution)/shard_map/dynamic_slice | solution.py:498
  3.9 0.1 pad_maximum_fusion.refs_4_
  4.0 0.0 copy-start
  4.0 0.8 %copy-done = bf16[256,128]{1,0:T(8,128)(2,1)S(1)} copy-done((bf16[256,128]{1,0:T(8,128)(2,1)S(1)}, bf16[256,128]{1,0:T(8,128)(2,1)}, u32[]{:S(2)}) %copy-start) | copy-done | bytes 65560
  4.8 0.0 copy-start.1
  4.8 0.8 %copy-done.1 = bf16[2,64,256]{2,1,0:T(8,128)(2,1)S(1)} copy-done((bf16[2,64,256]{2,1,0:T(8,128)(2,1)S(1)}, bf16[2,64,256]{2,1,0:T(8,128)(2,1)}, u32[]{:S(2)}) %copy-start.1) | copy-done | bytes 65560
  5.7 33.6 %gather_all.1 = (bf16[16,256,128]{2,1,0:T(8,128)(2,1)S(1)}, s32[16,8,256]{2,1,0:T(8,128)S(1)}, bf16[16,128,256]{2,1,0:T(8,128)(2,1)S(1)}) custom-call(bf16[256,128]{1,0:T(8,128)(2,1)S(1)} %copy-done, s32[8,256]{1,0:T(8,128)S(1)} %broadcast_in_dim.14.refs_1_, bf16[128,256]{1,0:T(8,128)(2,1)S(1)} %bitcast.17), custom_call_target="tpu_custom_call" | custom-call | tf_op jit(solution)/shard_map/gather_all/pallas_call | solution.py:238
  39.2 0.0 copy-start.2
  39.3 0.8 %copy-done.2 = bf16[128,256]{1,0:T(8,128)(2,1)S(1)} copy-done((bf16[128,256]{1,0:T(8,128)(2,1)S(1)}, bf16[128,256]{1,0:T(8,128)(2,1)}, u32[]{:S(2)}) %copy-start.2) | copy-done | bytes 65560
  40.1 0.0 copy-start.3
  40.1 0.7 copy-done.3
  40.8 22.4 %compute.1 = (f32[256,512]{1,0:T(8,128)}, f32[128,256]{1,0:T(8,128)S(1)}, f32[256,256]{1,0:T(8,128)S(1)}, f32[8,128]{1,0:T(8,128)S(1)}) custom-call(bf16[16,256,128]{2,1,0:T(8,128)(2,1)S(1)} %get-tuple-element.14.refs_0_, s32[16,8,256]{2,1,0:T(8,128)S(1)} %get-tuple-element.15.refs_1_, bf16[2048,256]{1,0:T(8,128)(2,1)S(1)} %bitcast.12, ...), custom_call_target="tpu_custom_call" | custom-call | tf_op jit(solution)/shard_map/compute/pallas_call | solution.py:451
  63.2 0.1 copy.13
  63.3 14.3 %finish.1 = (f32[16,8,256]{2,1,0:T(8,128)S(1)}, f32[8,128]{1,0:T(8,128)S(1)}, f32[2,64,256]{2,1,0:T(8,128)S(1)}) custom-call(f32[16,8,256]{2,1,0:T(8,128)S(1)} %bitcast.14, f32[8,128]{1,0:T(8,128)S(1)} %get-tuple-element.18.refs_1_, f32[8,2,8,256]{3,2,1,0:T(8,128)S(1)} %bitcast.13), custom_call_target="tpu_custom_call" | custom-call | tf_op jit(solution)/shard_map/finish/pallas_call | solution.py:330
  77.6 0.5 slice.3
  78.8 0.7 copy.16
  79.4 0.7 copy.17
  (2 shorter events, 0.0 us)
Async XLA Ops:
  4.0 0.8 %copy-start = (bf16[256,128]{1,0:T(8,128)(2,1)S(1)}, bf16[256,128]{1,0:T(8,128)(2,1)}, u32[]{:S(2)}) copy-start(bf16[256,128]{1,0:T(8,128)(2,1)} %refs_0_.1) | copy-start | bytes 196612
  4.8 0.8 %copy-start.1 = (bf16[2,64,256]{2,1,0:T(8,128)(2,1)S(1)}, bf16[2,64,256]{2,1,0:T(8,128)(2,1)}, u32[]{:S(2)}) copy-start(bf16[2,64,256]{2,1,0:T(8,128)(2,1)} %param.11) | copy-start | bytes 196612
  39.2 0.8 %copy-start.2 = (bf16[128,256]{1,0:T(8,128)(2,1)S(1)}, bf16[128,256]{1,0:T(8,128)(2,1)}, u32[]{:S(2)}) copy-start(bf16[128,256]{1,0:T(8,128)(2,1)} %refs_3_.1) | copy-start | bytes 196612
  40.1 0.7 copy-start.3

commit v4 on v3

--- a/solution.py
+++ b/solution.py
@@ -152,7 +152,10 @@
         return zz * 4 + xx * 2 + cc
 
     x_peer, core_peer = at(z, 1 - x, core), at(z, x, 1 - core)
-    greet([x_peer, core_peer] + [at((z + d) % depth, x, core) for d in range(1, depth)])
+    low, high = z % 2, z // 2
+    others = [(1 - low) + 2 * high, low + 2 * (1 - high), (1 - low) + 2 * (1 - high)]
+    z_peers = [at(zz, x, core) for zz in others]
+    greet([x_peer, core_peer] + z_peers)
 
     def copy(arr, source, block, peer, kind):
         return pltpu.make_async_remote_copy(
@@ -164,73 +167,44 @@
             device_id_type=MESH,
         )
 
+    started = []
+
+    def send(arr, block, peer, kind, source=None):
+        item = copy(arr, outs[arr].at[block] if source is None else source, block, peer, kind)
+        item.start()
+        started.append(item)
+
     def arrived(arr, block):
         copy(arr, outs[arr].at[block], block, core_peer, 0).wait_recv()
 
-    def spread(arr, zz, act, up, down, source=None):
-        block = at(zz, x, core)
-        source = outs[arr].at[block] if source is None else source
-
-        if up:
-
-            @pl.when(z < depth - 1)
-            def go_up():
-                act(copy(arr, source, block, at(z + 1, x, core), 2))
-
-        if down:
-
-            @pl.when(z > 0)
-            def go_down():
-                act(copy(arr, source, block, at(z - 1, x, core), 3))
-
-        act(copy(arr, source, block, x_peer, 0))
-        act(copy(arr, source, block, core_peer, 1))
-
-    def each_dist(fn):
-        for dist in range(1, depth):
-
-            @pl.when(z >= dist)
-            def below(dist=dist):
-                fn(z - dist, True, False)
-
-            @pl.when(z + dist < depth)
-            def above(dist=dist):
-                fn(z + dist, False, True)
-
-    begin = lambda item: item.start()
-    ended = lambda item: item.wait_send()
     own = []
     for arr in range(count):
-        spread(arr, z, begin, True, True, ins[arr])
+        for k, peer in enumerate(z_peers):
+            send(arr, me, peer, 2 + k, ins[arr])
+        send(arr, me, x_peer, 0, ins[arr])
+        send(arr, me, core_peer, 1, ins[arr])
         item = pltpu.make_async_copy(ins[arr], outs[arr].at[me], local_sem.at[arr])
         item.start()
         own.append(item)
-
     for arr in range(count):
-
-        def relay(zz, up, down):
-            arrived(arr, at(zz, x, core))
-            spread(arr, zz, begin, up, down)
-
-        each_dist(relay)
-
-        def across(zz, up=False, down=False):
+        arrived(arr, x_peer)
+        send(arr, x_peer, core_peer, 1)
+        for block in z_peers:
+            arrived(arr, block)
+            send(arr, block, x_peer, 0)
+            send(arr, block, core_peer, 1)
+    for arr in range(count):
+        for zz in others:
             block = at(zz, 1 - x, core)
             arrived(arr, block)
-            begin(copy(arr, outs[arr].at[block], block, core_peer, 1))
-
-        across(z)
-        each_dist(across)
+            send(arr, block, core_peer, 1)
     for arr in range(count):
-        for zz in range(depth):
+        for d in range(depth):
             for xx in range(2):
-                arrived(arr, at(zz, xx, 1 - core))
+                arrived(arr, at((z + d) % depth, xx, 1 - core))
         own[arr].wait()
-        spread(arr, z, ended, True, True, ins[arr])
-        each_dist(lambda zz, up, down: spread(arr, zz, ended, up, down))
-        for zz in range(depth):
-            block = at(zz, 1 - x, core)
-            ended(copy(arr, outs[arr].at[block], block, core_peer, 1))
+    for item in started:
+        item.wait_send()
 
 
 def gather_all(n, arrays):
@@ -241,7 +215,7 @@
         in_specs=[VMEM] * count,
         out_specs=[VMEM] * count,
         scratch_shapes=[
-            pltpu.SemaphoreType.DMA((count, n, 4)),
+            pltpu.SemaphoreType.DMA((count, n, 1 + n // 4)),
             pltpu.SemaphoreType.DMA((count, n)),
             pltpu.SemaphoreType.DMA((count,)),
         ],

time: 81.6 us -> 73.4 us (0.90)
  Pallas kernels: 70.3 us -> 62.1 us
    pallas_call x1, Pallas kernels: 33.6 us -> 25.3 us  [gather_all(): pl.pallas_call(lambda *refs: gather_kernel(n, count, *refs), out_shape=[j...]
where the time goes in v4:
time: 73.4 us; the launch traced here: 73.1 us
  Pallas kernels  62.1 us (85%)
  local copies, waits for them, and re-layouts  6.29 us (9%)
  between operations  2.51 us (3%)
  other arithmetic  2.13 us (3%)
    pallas_call x1, Pallas kernels, gather_all(): pl.pallas_call(lambda *refs: gather_kernel(n, count, *refs), out_shape=[j...  25.3 us
    pallas_call x1, Pallas kernels, compute(): pl.pallas_call(lambda *refs: compute_kernel(n, blocks, a_count, *refs), o...  22.4 us
    pallas_call x1, Pallas kernels, finish(): pl.pallas_call(lambda *refs: finish_kernel(n, *refs), out_shape=[jax.Shap...  14.5 us
    unnamed x11, local copies, waits for them, and re-layouts  4.58 us

profile of v4, /device:TPU:0, one launch (start us, length us, event | category | flops | bytes accessed | tf_op | source)
XLA Modules:
  0.0 73.1 jit_solution(11069840633434264249)
XLA Ops:
  0.7 0.7 select_multiply_fusion
  1.4 0.7 broadcast_multiply_fusion
  2.0 0.7 add_add_fusion
  2.7 1.2 %constant_dynamic-slice_fusion.1 = (bf16[256,512]{1,0:T(8,128)(2,1)S(1)}, bf16[256,512]{1,0:T(8,128)(2,1)S(1)}, bf16[256,512]{1,0:T(8,128)(2,1)S(1)}) fusion(bf16[256,8192]{1,0:T(8,128)(2,1)} %param.10, s32[]{:T(128)S(6)} %select_n.34, s32[]{:T(128)S(6)} %select_n.32, s32[]{:T(128)S(6)} %select_n.33), kind=kLoop, calls=%fused_computation.3 | loop fusion | bytes 1572876 | tf_op jit(solution)/shard_map/dynamic_slice | solution.py:472
  3.9 0.1 pad_maximum_fusion.refs_4_
  4.0 0.0 copy-start
  4.0 0.8 %copy-done = bf16[256,128]{1,0:T(8,128)(2,1)S(1)} copy-done((bf16[256,128]{1,0:T(8,128)(2,1)S(1)}, bf16[256,128]{1,0:T(8,128)(2,1)}, u32[]{:S(2)}) %copy-start) | copy-done | bytes 65560
  4.8 0.0 copy-start.1
  4.8 0.8 %copy-done.1 = bf16[2,64,256]{2,1,0:T(8,128)(2,1)S(1)} copy-done((bf16[2,64,256]{2,1,0:T(8,128)(2,1)S(1)}, bf16[2,64,256]{2,1,0:T(8,128)(2,1)}, u32[]{:S(2)}) %copy-start.1) | copy-done | bytes 65560
  5.7 25.3 %gather_all.1 = (bf16[16,256,128]{2,1,0:T(8,128)(2,1)S(1)}, s32[16,8,256]{2,1,0:T(8,128)S(1)}, bf16[16,128,256]{2,1,0:T(8,128)(2,1)S(1)}) custom-call(bf16[256,128]{1,0:T(8,128)(2,1)S(1)} %copy-done, s32[8,256]{1,0:T(8,128)S(1)} %broadcast_in_dim.14.refs_1_, bf16[128,256]{1,0:T(8,128)(2,1)S(1)} %bitcast.17), custom_call_target="tpu_custom_call" | custom-call | tf_op jit(solution)/shard_map/gather_all/pallas_call | solution.py:212
  30.9 0.0 copy-start.2
  31.0 0.8 %copy-done.2 = bf16[128,256]{1,0:T(8,128)(2,1)S(1)} copy-done((bf16[128,256]{1,0:T(8,128)(2,1)S(1)}, bf16[128,256]{1,0:T(8,128)(2,1)}, u32[]{:S(2)}) %copy-start.2) | copy-done | bytes 65560
  31.8 0.0 copy-start.3
  31.8 0.7 copy-done.3
  32.5 22.4 %compute.1 = (f32[256,512]{1,0:T(8,128)}, f32[128,256]{1,0:T(8,128)S(1)}, f32[256,256]{1,0:T(8,128)S(1)}, f32[8,128]{1,0:T(8,128)S(1)}) custom-call(bf16[16,256,128]{2,1,0:T(8,128)(2,1)S(1)} %get-tuple-element.14.refs_0_, s32[16,8,256]{2,1,0:T(8,128)S(1)} %get-tuple-element.15.refs_1_, bf16[2048,256]{1,0:T(8,128)(2,1)S(1)} %bitcast.12, ...), custom_call_target="tpu_custom_call" | custom-call | tf_op jit(solution)/shard_map/compute/pallas_call | solution.py:425
  54.9 0.1 copy.13
  55.0 14.5 %finish.1 = (f32[16,8,256]{2,1,0:T(8,128)S(1)}, f32[8,128]{1,0:T(8,128)S(1)}, f32[2,64,256]{2,1,0:T(8,128)S(1)}) custom-call(f32[16,8,256]{2,1,0:T(8,128)S(1)} %bitcast.14, f32[8,128]{1,0:T(8,128)S(1)} %get-tuple-element.18.refs_1_, f32[8,2,8,256]{3,2,1,0:T(8,128)S(1)} %bitcast.13), custom_call_target="tpu_custom_call" | custom-call | tf_op jit(solution)/shard_map/finish/pallas_call | solution.py:304
  69.4 0.5 slice.3
  70.6 0.7 copy.16
  71.3 0.7 copy.17
  (2 shorter events, 0.0 us)
Async XLA Ops:
  4.0 0.8 %copy-start = (bf16[256,128]{1,0:T(8,128)(2,1)S(1)}, bf16[256,128]{1,0:T(8,128)(2,1)}, u32[]{:S(2)}) copy-start(bf16[256,128]{1,0:T(8,128)(2,1)} %refs_0_.1) | copy-start | bytes 196612
  4.8 0.8 %copy-start.1 = (bf16[2,64,256]{2,1,0:T(8,128)(2,1)S(1)}, bf16[2,64,256]{2,1,0:T(8,128)(2,1)}, u32[]{:S(2)}) copy-start(bf16[2,64,256]{2,1,0:T(8,128)(2,1)} %param.11) | copy-start | bytes 196612
  30.9 0.8 %copy-start.2 = (bf16[128,256]{1,0:T(8,128)(2,1)S(1)}, bf16[128,256]{1,0:T(8,128)(2,1)}, u32[]{:S(2)}) copy-start(bf16[128,256]{1,0:T(8,128)(2,1)} %refs_3_.1) | copy-start | bytes 196612
  31.8 0.7 copy-start.3
